TPU v7x, 256 devices: a whole 4x4x8 slice. The times are simulated.
256 devices in a mesh: row: 64 (over y, z, core), col: 4 (over x).
Axes of the slice: x: 4, y: 4, z: 8, core: 2. Of those that a mesh axis runs over, the one named last changes fastest.
Arguments:
- entity_feats: bfloat16 [65536, 256], P(('col', 'row')), may hold values from -6 to 6
- class_map: int32 [65536], P(('col', 'row')), may hold values from 0 to 127, as said below
- tile_values: bfloat16 [8192, 128, 128], P(('row', 'col')), may hold values from -0.09375 to 0.09375
- tile_rows: int32 [8192], P(('row', 'col')), may hold values from 0 to 3
- tile_column_index: int32 [8192], P(('row', 'col')), may hold values from 0 to 63
- tile_rels: int32 [8192], P(('row', 'col')), may hold values from 0 to 499
- tile_counts: int32 [256], P(('row', 'col')), may hold values from 4 to 32, as said below
- coefficients: bfloat16 [500, 8], replicated, may hold values from -2 to 2
- bases: bfloat16 [8, 256, 256], replicated, may hold values from -0.375 to 0.375
- cotangent: bfloat16 [32768, 256], P(('row', 'col')), may hold values from -6 to 6
Outputs:
- layer_out: bfloat16 [32768, 256], P(('row', 'col'))
- grad_entities: float32 [65536, 256], P(('col', 'row'))
- grad_bases: float32 [8, 256, 256], replicated
- grad_coef: float32 [500, 8], replicated
Inputs may be any that keep to these rules, and one draw needn't show every extreme that they name: `class_map`: within every block of 256 entities, every class number 0 to 127 occurs at least once. `tile_counts`: tile slots of a device from its count onward are unused; some device has all 32 slots live in every draw.
All inputs are finite; a program needn't handle non-finite values.
Results may differ from a plain program's by a relative error of at most 0.006.
Values may be sent and summed in bfloat16 or wider, within the bound.
No kernel may reach another device: no remote copies, remote signals or barrier semaphores. Data moves between devices by JAX's collectives and lax.ppermute only.
A program may use at most 128 MiB of HBM per device.

v0:
```python
import jax
import jax.numpy as jnp
from jax import lax
from jax.sharding import PartitionSpec as P

TBLK = 32


def tile_weights(rel_block, row_block, live, coefficients, trows, relations):
    pick_rel = (rel_block[:, None] == jnp.arange(relations, dtype=jnp.int32)[None, :]).astype(
        jnp.bfloat16
    )
    coef_rows = jnp.dot(pick_rel, coefficients, preferred_element_type=jnp.float32)
    pick_row = (
        (row_block[:, None] == jnp.arange(trows, dtype=jnp.int32)[None, :]) & live[:, None]
    ).astype(jnp.float32)
    weights = (pick_row[:, :, None] * coef_rows[:, None, :]).astype(jnp.bfloat16)
    return (weights, pick_row)


def local(
    entity_feats,
    class_map,
    tile_values,
    tile_rows,
    tile_column_index,
    tile_rels,
    tile_counts,
    coefficients,
    bases,
    cotangent,
):
    n_row = lax.axis_size("row")
    n_col = lax.axis_size("col")
    node_dev = cotangent.shape[0]
    tile = tile_values.shape[1]
    nbases = bases.shape[0]
    width = bases.shape[1]
    relations = coefficients.shape[0]
    rblock = node_dev * n_col
    cblock = node_dev * n_row
    trows = rblock // tile
    tile_column_list = cblock // tile
    member = class_map[:, None] == jnp.arange(node_dev, dtype=jnp.int32)[None, :]
    member_bf = member.astype(jnp.bfloat16)
    sums = lax.dot_general(
        member_bf, entity_feats, (((0,), (0,)), ((), ())), preferred_element_type=jnp.float32
    )
    counts = jnp.sum(member.astype(jnp.float32), axis=0)
    class_feat = (sums / counts[:, None]).astype(jnp.bfloat16)
    sender_device = lax.all_gather(class_feat, "row", axis=0, tiled=True).reshape(
        tile_column_list, tile, width
    )
    stacked = bases.reshape(nbases * width, width)
    live_count = tile_counts[0]
    turns = (live_count + TBLK - 1) // TBLK

    def forward_turn(step, carry):
        sums_acc, msg_store = carry
        leading_entry = step * TBLK
        live = leading_entry + jnp.arange(TBLK, dtype=jnp.int32) < live_count
        selected_entries = jnp.take(sender_device, tile_column_index, axis=0)
        messages = jnp.einsum(
            "kij,kjh->kih", tile_values, selected_entries, preferred_element_type=jnp.float32
        ).astype(jnp.bfloat16)
        weights, pick_row = tile_weights(tile_rels, tile_rows, live, coefficients, trows, relations)
        sums_acc = sums_acc + jnp.einsum(
            "ktb,kih->tibh", weights, messages, preferred_element_type=jnp.float32
        )
        msg_store = messages
        return (sums_acc, msg_store)

    init_sums = jnp.zeros((trows, tile, nbases, width), jnp.float32)
    init_store = jnp.zeros((tile_values.shape[0], tile, width), jnp.bfloat16)
    sums_acc, msg_store = lax.fori_loop(0, turns, forward_turn, (init_sums, init_store))
    part = sums_acc.astype(jnp.bfloat16).reshape(rblock, nbases * width)
    out_part = jnp.dot(part, stacked, preferred_element_type=jnp.float32)
    layer_out = lax.psum_scatter(out_part, "col", scatter_dimension=0, tiled=True).astype(
        jnp.bfloat16
    )
    dout_rows = lax.all_gather(cotangent, "col", axis=0, tiled=True)
    grads_rows = lax.dot_general(
        dout_rows, stacked, (((1,), (1,)), ((), ())), preferred_element_type=jnp.float32
    ).astype(jnp.bfloat16)
    dv_part = lax.dot_general(
        part, dout_rows, (((0,), (0,)), ((), ())), preferred_element_type=jnp.float32
    )
    grads_tiles = grads_rows.reshape(trows, tile, nbases, width)

    def backward_turn(step, carry):
        dcoef_acc, dx_acc = carry
        leading_entry = step * TBLK
        live = leading_entry + jnp.arange(TBLK, dtype=jnp.int32) < live_count
        weights, pick_row = tile_weights(tile_rels, tile_rows, live, coefficients, trows, relations)
        gram = jnp.einsum(
            "kih,tibh->ktb", msg_store, grads_tiles, preferred_element_type=jnp.float32
        )
        per_tile = jnp.sum(gram * pick_row[:, :, None], axis=1)
        dcoef_acc = dcoef_acc + jax.ops.segment_sum(per_tile, tile_rels, num_segments=relations)
        mixed = jnp.einsum(
            "ktb,tibh->kih", weights, grads_tiles, preferred_element_type=jnp.float32
        ).astype(jnp.bfloat16)
        back = jnp.einsum("kij,kih->kjh", tile_values, mixed, preferred_element_type=jnp.float32)
        dx_acc = dx_acc.at[tile_column_index].add(back)
        return (dcoef_acc, dx_acc)

    init_coef = jnp.zeros((relations, nbases), jnp.float32)
    init_dx = jnp.zeros((tile_column_list, tile, width), jnp.float32)
    dcoef_acc, dx_acc = lax.fori_loop(0, turns, backward_turn, (init_coef, init_dx))
    dx_all = dx_acc.reshape(cblock, width)
    dx_own = lax.psum_scatter(dx_all, "row", scatter_dimension=0, tiled=True)
    dv_sum, dcoef_sum = lax.psum((dv_part, dcoef_acc), ("row", "col"))
    scale = (node_dev * n_row * n_col) ** (-0.5)
    grad_bases = (dv_sum * scale).reshape(nbases, width, width)
    grad_coef = dcoef_sum * scale
    quotient = dx_own / counts[:, None]
    grad_entities = jnp.dot(member.astype(jnp.float32), quotient, precision=lax.Precision.HIGHEST)
    return (layer_out, grad_entities, grad_bases, grad_coef)


def solution(mesh):
    placed = (
        P(("col", "row"), None),
        P(("col", "row")),
        P(("row", "col"), None, None),
        P(("row", "col")),
        P(("row", "col")),
        P(("row", "col")),
        P(("row", "col")),
        P(),
        P(),
        P(("row", "col"), None),
    )
    return jax.shard_map(
        local,
        mesh=mesh,
        in_specs=placed,
        out_specs=(P(("row", "col"), None), P(("col", "row"), None), P(), P()),
        check_vma=False,
    )
```

profile of v0, /device:TPU:2, one launch (start us, length us, event | category | flops | bytes accessed | tf_op | source)
XLA Modules:
  0.0 570.0 jit_solution(12668102719578885372)
XLA Ops:
  8.1 1.8 fusion.22
  10.7 12.6 %all_gather.7 = bf16[512,256]{1,0:T(8,128)(2,1)S(1)} all-gather(bf16[128,256]{1,0:T(8,128)(2,1)} %param.23), channel_id=1, replica_groups=mesh['row'=64,'col'=4] {'col'}, dimensions={0}, use_global_device_ids=true | all-gather | bytes 327680 | tf_op jit(solution)/shard_map/all_gather | solution.py:81
  25.5 67.9 %all-gather.2.cloned.1.call-done = bf16[8192,256]{1,0:T(8,128)(2,1)} async-done(((bf16[128,256]{1,0:T(8,128)(2,1)}), bf16[8192,256]{1,0:T(8,128)(2,1)}) %all-gather.2.cloned.1.call-update) | async-done | bytes 4194320 | tf_op jit(solution)/shard_map/all_gather | solution.py:51
  93.4 4.3 gather_fusion
  97.7 3.8 convert_bitcast_fusion
  101.4 3.4 copy.35
  104.8 1.6 broadcast_in_dim.33
  106.4 2.3 broadcast_in_dim.32
  108.7 6.6 %while.31 = (s32[]{:T(128)}, f32[4,128,8,256]{3,2,1,0:T(8,128)}, bf16[32,128,256]{2,0,1:T(8,128)(2,1)}, s32[]{:T(128)}, s32[32]{0:T(128)S(1)}, /*index=5*/s32[]{...) while((s32[]{:T(128)}, f32[4,128,8,256]{3,2,1,0:T(8,128)}, ...), condition=%wide.region_2.3_spmd, body=%wide.region_1.2_spmd.sunk | while | flops 68159936 | bytes 48236912 | solution.py:75
  110.7 1.6 copy-done.1
  113.4 1.9 copy-done.2
  115.3 2.4 convert_element_type.73
  119.8 2.1 fusion.37
  128.2 4.3 broadcast_in_dim.46
  132.4 22.2 %while.32 = (s32[]{:T(128)}, f32[500,8]{1,0:T(8,128)S(1)}, f32[64,128,256]{2,1,0:T(8,128)}, s32[]{:T(128)}, s32[32]{0:T(128)S(1)}, /*index=5*/s32[32]{0:T(128)S(...) while((s32[]{:T(128)}, f32[500,8]{1,0:T(8,128)S(1)}, ...), condition=%wide.region_8.9_spmd, body=%wide.region_4.8_spmd.sunk | while | flops 337646112 | bytes 36713844 | solution.py:109
  135.3 3.7 convolution_bitcast_fusion.2
  139.0 5.6 copy.51
  144.6 10.1 %scatter_fusion.1 = f32[64,128,256]{2,1,0:T(8,128)} fusion(f32[64,128,256]{2,1,0:T(8,128)} %get-tuple-element.645, s32[32]{0:T(128)S(1)} %fusion.66, f32[32,128,256]{2,1,0:T(8,128)} %copy.51), kind=kCustom, calls=%fused_computation.2.clone.1 | custom fusion | flops 1048576 | bytes 12583040 | tf_op jit(solution)/shard_map/while/body/scatter-add | solution.py:104
  154.8 75.1 %psum.15 = f32[500,8]{0,1:T(8,128)S(1)} all-reduce(f32[500,8]{0,1:T(8,128)S(1)} %copy.37), channel_id=1, replica_groups=mesh['row'=64,'col'=4] {'row','col'}, use_global_device_ids=true, to_apply=%region_11.12 | all-reduce | flops 4000 | bytes 32000 | tf_op jit(solution)/shard_map/psum | solution.py:112
  230.5 150.1 %all-reduce.2.cloned.1.call-done = f32[2048,256]{1,0:T(8,128)} async-done(((f32[2048,256]{1,0:T(8,128)}), f32[2048,256]{1,0:T(8,128)}) %all-reduce.2.cloned.1.call-update) | async-done | bytes 2097168 | tf_op jit(solution)/shard_map/psum | solution.py:112
  380.6 3.1 broadcast_multiply_fusion
  383.7 20.1 %reduce-scatter.3.cloned.1.call-done = f32[128,256]{1,0:T(8,128)} async-done(((f32[512,256]{1,0:T(8,128)}), f32[128,256]{1,0:T(8,128)}) %reduce-scatter.3.cloned.1.call-update) | async-done | bytes 131088 | tf_op jit(solution)/shard_map/reduce_scatter | solution.py:78
  405.3 156.1 %reduce-scatter.5.cloned.1.call-done = f32[128,256]{1,0:T(8,128)} async-done(((f32[8192,256]{1,0:T(8,128)}), f32[128,256]{1,0:T(8,128)}) %reduce-scatter.5.cloned.1.call-update) | async-done | bytes 131088 | tf_op jit(solution)/shard_map/reduce_scatter | solution.py:111
  561.5 2.0 fusion.27
  (56 shorter events, 19.6 us)
Async XLA Ops:
  7.2 114.7 %copy-start = (bf16[8,256,256]{2,1,0:T(8,128)(2,1)S(1)}, bf16[8,256,256]{2,1,0:T(8,128)(2,1)}, u32[]{:S(2)}) copy-start(bf16[8,256,256]{2,1,0:T(8,128)(2,1)} %param.22) | copy-start | bytes 3145732
  7.2 86.2 %all-gather.2.cloned.1.call-start = ((), (), s32[]{:S(2)}) async-start(), calls=%async_computation.2 | async-start | bytes 4259840 | tf_op jit(solution)/shard_map/all_gather | solution.py:51
  10.0 370.7 %all-reduce.2.cloned.1.call-start = ((), (), s32[]{:S(2)}) async-start(), calls=%async_computation.5 | async-start | bytes 4194304 | tf_op jit(solution)/shard_map/psum | solution.py:112
  93.4 4.3 copy-start.3
  106.4 2.3 copy-start.8
  109.4 2.9 copy-start.1
  113.4 1.9 copy-start.2
  118.4 1.3 copy-start.5
  121.9 282.0 %reduce-scatter.3.cloned.1.call-start = ((), (), s32[]{:S(2)}) async-start(), calls=%async_computation.3 | async-start | bytes 655360 | tf_op jit(solution)/shard_map/reduce_scatter | solution.py:78
  123.3 1.6 copy-start.7
  124.9 1.6 copy-start.6
  128.1 433.4 %reduce-scatter.5.cloned.1.call-start = ((), (), s32[]{:S(2)}) async-start(), calls=%async_computation.4 | async-start | bytes 8519680 | tf_op jit(solution)/shard_map/reduce_scatter | solution.py:111
  128.2 4.3 copy-start.9
  128.2 4.3 copy-start.11
  134.1 1.2 copy-start.4
  230.5 331.0 %copy-start.10 = (s32[256]{0:T(256)S(1)}, s32[256]{0:T(256)}, u32[]{:S(2)}) copy-start(s32[256]{0:T(256)} %param.15) | copy-start | bytes 3076
Sparse Core Ops, SparseCore 0:
  11.4 81.9 all-gather.1
  122.0 258.6 all-reduce.1
  383.2 20.6 reduce-scatter.2
  407.9 153.5 reduce-scatter.4
where the time goes:
time: 571 us; the launch traced here: 570 us
  waiting for transfers between devices  394 us (69%)
  blocking collectives  87.6 us (15%)
  local copies, waits for them, and re-layouts  32.2 us (6%)
  other arithmetic  22.1 us (4%)
  matrix products  18.9 us (3%)
  between operations  14.5 us (3%)
    reduce_scatter x1, waiting for transfers between devices, local(): dx_own = lax.psum_scatter(dx_all, 'row', scatter_dimension=0, tiled=True)  156 us
    psum x1, waiting for transfers between devices, local(): dv_sum, dcoef_sum = lax.psum((dv_part, dcoef_acc), ('row', 'col'))  150 us
    psum x1, blocking collectives, local(): dv_sum, dcoef_sum = lax.psum((dv_part, dcoef_acc), ('row', 'col'))  75.1 us
    all_gather x1, waiting for transfers between devices, local(): lax.all_gather(class_feat, 'row', axis=0, tiled=True)  67.9 us
    reduce_scatter x1, waiting for transfers between devices, local(): lax.psum_scatter(out_part, 'col', scatter_dimension=0, tiled=True)  20.1 us
    all_gather x1, blocking collectives, local(): dout_rows = lax.all_gather(cotangent, 'col', axis=0, tiled=True)  12.6 us
  transfers between devices with their start and end apart: 4, of which 4 were waited for; matrix products, arithmetic and copies ran while one was open for 7% of the time, Pallas kernels for 0%

commit v1 on v0

--- a/solution.py
+++ b/solution.py
@@ -48,9 +48,9 @@
     )
     counts = jnp.sum(member.astype(jnp.float32), axis=0)
     class_feat = (sums / counts[:, None]).astype(jnp.bfloat16)
-    sender_device = lax.all_gather(class_feat, "row", axis=0, tiled=True).reshape(
-        tile_column_list, tile, width
-    )
+    sender_device = jnp.concatenate(
+        lax.all_to_all(jnp.stack([class_feat] * lax.axis_size("row")), "row", 0, 0), axis=0
+    ).reshape(tile_column_list, tile, width)
     stacked = bases.reshape(nbases * width, width)
     live_count = tile_counts[0]
     turns = (live_count + TBLK - 1) // TBLK

time: 571 us -> 426 us (0.75)
  waiting for transfers between devices: 394 us -> 236 us
  starting transfers between devices: 0.16 us -> 12.6 us
    reduce_scatter x1, waiting for transfers between devices: 156 us -> 0.01 us  [local(): dx_own = lax.psum_scatter(dx_all, 'row', scatter_dimension=0, tiled=True)]
    all_to_all x0 -> x1, waiting for transfers between devices: none -> 82.4 us  [local(): lax.all_to_all(jnp.stack([class_feat] * lax.axis_size('row')), 'row', 0, 0)]
    all_gather x1 -> x0, waiting for transfers between devices: 67.9 us -> none  [local(): lax.all_gather(class_feat, 'row', axis=0, tiled=True)]
    reduce_scatter x1, waiting for transfers between devices: 20.1 us -> 0.01 us  [local(): lax.psum_scatter(out_part, 'col', scatter_dimension=0, tiled=True)]
    all_to_all x0 -> x1, starting transfers between devices: none -> 12.5 us  [local(): lax.all_to_all(jnp.stack([class_feat] * lax.axis_size('row')), 'row', 0, 0)]
  transfers between devices with their start and end apart: 4 -> 4, of which waited for: 4 -> 2; matrix products, arithmetic and copies ran while one was open for 7% -> 8% of each run, Pallas kernels for 0% -> 0%
where the time goes in v1:
time: 426 us; the launch traced here: 425 us
  waiting for transfers between devices  236 us (55%)
  blocking collectives  86.7 us (20%)
  local copies, waits for them, and re-layouts  34.6 us (8%)
  other arithmetic  20.9 us (5%)
  matrix products  17.6 us (4%)
  between operations  16.3 us (4%)
  starting transfers between devices  12.6 us (3%)
    psum x1, waiting for transfers between devices, local(): dv_sum, dcoef_sum = lax.psum((dv_part, dcoef_acc), ('row', 'col'))  154 us
    all_to_all x1, waiting for transfers between devices, local(): lax.all_to_all(jnp.stack([class_feat] * lax.axis_size('row')), 'row', 0, 0)  82.4 us
    psum x1, blocking collectives, local(): dv_sum, dcoef_sum = lax.psum((dv_part, dcoef_acc), ('row', 'col'))  74.4 us
    all_to_all x1, starting transfers between devices, local(): lax.all_to_all(jnp.stack([class_feat] * lax.axis_size('row')), 'row', 0, 0)  12.5 us
    all_gather x1, blocking collectives, local(): dout_rows = lax.all_gather(cotangent, 'col', axis=0, tiled=True)  12.3 us
    scatter-add x1, other arithmetic, backward_turn(): dx_acc = dx_acc.at[tile_column_index].add(back)  10.2 us
  transfers between devices with their start and end apart: 4, of which 2 were waited for; matrix products, arithmetic and copies ran while one was open for 8% of the time, Pallas kernels for 0%

profile of v1, /device:TPU:2, one launch (start us, length us, event | category | flops | bytes accessed | tf_op | source)
XLA Modules:
  0.0 425.3 jit_solution(12187946912423753669)
XLA Ops:
  10.1 2.5 stack.2
  12.6 12.5 %all-to-all-start = ((bf16[64,128,256]{2,1,0:T(8,128)(2,1)}), bf16[64,128,256]{2,1,0:T(8,128)(2,1)}, u32[]{:S(2)}, u32[]{:S(2)}) async-start(bf16[64,128,256]{2,1,0:T(8,128)(2,1)} %stack.2), calls=%async_computation | async-start | bytes 8388608 | tf_op jit(solution)/shard_map/all_to_all | solution.py:52
  25.8 12.3 %all_gather.3 = bf16[512,256]{1,0:T(8,128)(2,1)S(1)} all-gather(bf16[128,256]{1,0:T(8,128)(2,1)S(1)} %copy-done.8), channel_id=1, replica_groups=mesh['row'=64,'col'=4] {'col'}, dimensions={0}, use_global_device_ids=true | all-gather | bytes 327680 | tf_op jit(solution)/shard_map/all_gather | solution.py:81
  38.4 82.4 %all-to-all-done = bf16[64,128,256]{2,1,0:T(8,128)(2,1)} async-done(((bf16[64,128,256]{2,1,0:T(8,128)(2,1)}), bf16[64,128,256]{2,1,0:T(8,128)(2,1)}, u32[]{:S(2)}, u32[]{:S(2)}) %all-to-all-start) | async-done | bytes 4194336 | tf_op jit(solution)/shard_map/all_to_all | solution.py:52
  120.8 4.2 gather_fusion
  125.0 3.8 convert_bitcast_fusion
  128.8 3.4 copy.35
  132.2 1.6 broadcast_in_dim.33
  133.7 2.3 broadcast_in_dim.32
  136.1 6.6 %while.31 = (s32[]{:T(128)}, f32[4,128,8,256]{3,2,1,0:T(8,128)}, bf16[32,128,256]{2,0,1:T(8,128)(2,1)}, s32[]{:T(128)}, s32[32]{0:T(128)S(1)}, /*index=5*/s32[]{...) while((s32[]{:T(128)}, f32[4,128,8,256]{3,2,1,0:T(8,128)}, ...), condition=%wide.region_2.3_spmd, body=%wide.region_1.2_spmd.sunk | while | flops 68159936 | bytes 48236912 | solution.py:75
  138.1 1.6 copy-done.1
  140.7 1.9 copy-done.2
  142.7 2.4 convert_element_type.73
  147.1 2.1 fusion.37
  155.5 4.3 broadcast_in_dim.46
  159.7 22.3 %while.32 = (s32[]{:T(128)}, f32[500,8]{1,0:T(8,128)S(1)}, f32[64,128,256]{2,1,0:T(8,128)}, s32[]{:T(128)}, s32[32]{0:T(128)S(1)}, /*index=5*/s32[32]{0:T(128)S(...) while((s32[]{:T(128)}, f32[500,8]{1,0:T(8,128)S(1)}, ...), condition=%wide.region_8.9_spmd, body=%wide.region_4.8_spmd.sunk | while | flops 337646112 | bytes 36713844 | solution.py:109
  162.6 3.6 convolution_bitcast_fusion.2
  166.3 5.6 %copy.51 = f32[32,128,256]{2,1,0:T(8,128)} copy(f32[32,128,256]{1,2,0:T(8,128)} %convolution_bitcast_fusion.2) | data formatting | bytes 8388608 | tf_op jit(solution)/shard_map/while/body/kij,kih->kjh/dot_general | solution.py:103
  171.9 10.2 %scatter_fusion.1 = f32[64,128,256]{2,1,0:T(8,128)} fusion(f32[64,128,256]{2,1,0:T(8,128)} %get-tuple-element.645, s32[32]{0:T(128)S(1)} %fusion.66, f32[32,128,256]{2,1,0:T(8,128)} %copy.51), kind=kCustom, calls=%fused_computation.2.clone.1 | custom fusion | flops 1048576 | bytes 12583040 | tf_op jit(solution)/shard_map/while/body/scatter-add | solution.py:104
  182.2 74.4 %psum.15 = f32[500,8]{0,1:T(8,128)S(1)} all-reduce(f32[500,8]{0,1:T(8,128)S(1)} %copy.37), channel_id=1, replica_groups=mesh['row'=64,'col'=4] {'row','col'}, use_global_device_ids=true, to_apply=%region_11.12 | all-reduce | flops 4000 | bytes 32000 | tf_op jit(solution)/shard_map/psum | solution.py:112
  257.2 154.0 %all-reduce.2.cloned.1.call-done = f32[2048,256]{1,0:T(8,128)} async-done(((f32[2048,256]{1,0:T(8,128)}), f32[2048,256]{1,0:T(8,128)}) %all-reduce.2.cloned.1.call-update) | async-done | bytes 2097168 | tf_op jit(solution)/shard_map/psum | solution.py:112
  411.3 3.1 broadcast_multiply_fusion
  414.4 1.5 convert_element_type.74
  415.9 2.0 fusion.27
  (60 shorter events, 17.2 us)
Async XLA Ops:
  8.0 141.2 %copy-start = (bf16[8,256,256]{2,1,0:T(8,128)(2,1)S(1)}, bf16[8,256,256]{2,1,0:T(8,128)(2,1)}, u32[]{:S(2)}) copy-start(bf16[8,256,256]{2,1,0:T(8,128)(2,1)} %param.22) | copy-start | bytes 3145732
  12.6 13.3 %copy-start.8 = (bf16[128,256]{1,0:T(8,128)(2,1)S(1)}, bf16[128,256]{1,0:T(8,128)(2,1)}, u32[]{:S(2)}) copy-start(bf16[128,256]{1,0:T(8,128)(2,1)} %param.23) | copy-start | bytes 196612
  12.6 25.6 %copy-start.13 = (s32[32]{0:T(128)S(1)}, s32[32]{0:T(128)}, u32[]{:S(2)}) copy-start(s32[32]{0:T(128)} %param.18) | copy-start | bytes 388
  12.6 25.6 %copy-start.10 = (s32[32]{0:T(128)S(1)}, s32[32]{0:T(128)}, u32[]{:S(2)}) copy-start(s32[32]{0:T(128)} %param.19) | copy-start | bytes 388
  12.6 25.6 %copy-start.11 = (bf16[500,8]{0,1:T(8,128)(2,1)S(1)}, bf16[500,8]{0,1:T(8,128)(2,1)}, u32[]{:S(2)}) copy-start(bf16[500,8]{0,1:T(8,128)(2,1)} %param.21) | copy-start | bytes 24004
  12.6 108.2 %all-to-all-start = ((bf16[64,128,256]{2,1,0:T(8,128)(2,1)}), bf16[64,128,256]{2,1,0:T(8,128)(2,1)}, u32[]{:S(2)}, u32[]{:S(2)}) async-start(bf16[64,128,256]{2,1,0:T(8,128)(2,1)} %stack.2), calls=%async_computation | async-start | bytes 8388608 | tf_op jit(solution)/shard_map/all_to_all | solution.py:52
  25.1 386.2 %all-reduce.2.cloned.1.call-start = ((), (), s32[]{:S(2)}) async-start(), calls=%async_computation.5 | async-start | bytes 4194304 | tf_op jit(solution)/shard_map/psum | solution.py:112
  38.4 86.6 %copy-start.3 = (bf16[32,128,128]{2,1,0:T(8,128)(2,1)S(1)}, bf16[32,128,128]{2,1,0:T(8,128)(2,1)}, u32[]{:S(2)}) copy-start(bf16[32,128,128]{2,1,0:T(8,128)(2,1)} %param.16) | copy-start | bytes 3145732
  133.7 2.3 copy-start.9
  136.7 2.9 copy-start.1
  140.7 1.9 copy-start.2
  145.8 1.3 copy-start.5
  149.2 265.2 %reduce-scatter.3.cloned.1.call-start = ((), (), s32[]{:S(2)}) async-start(), calls=%async_computation.3 | async-start | bytes 655360 | tf_op jit(solution)/shard_map/reduce_scatter | solution.py:78
  150.7 1.6 copy-start.7
  152.3 1.6 copy-start.6
  155.4 260.5 %reduce-scatter.5.cloned.1.call-start = ((), (), s32[]{:S(2)}) async-start(), calls=%async_computation.4 | async-start | bytes 8519680 | tf_op jit(solution)/shard_map/reduce_scatter | solution.py:111
  161.4 1.2 copy-start.4
  257.2 158.7 %copy-start.12 = (s32[256]{0:T(256)S(1)}, s32[256]{0:T(256)}, u32[]{:S(2)}) copy-start(s32[256]{0:T(256)} %param.15) | copy-start | bytes 3076
Sparse Core Ops, SparseCore 0:
  149.3 261.9 all-reduce.1
Sparse Core Ops, SparseCore 1:
  155.5 18.7 reduce-scatter.2
  182.2 149.3 reduce-scatter.4
